TPU v7x, 256 devices: a whole 4x4x8 slice. The times are simulated.
256 devices in a mesh: tx: 16 (over y_lo, z), ty: 16 (over y_hi, x, core).
Axes of the slice: x: 4, y: 4 (y_hi: 2, y_lo: 2; y = y_hi * 2 + y_lo), z: 8, core: 2. Of those that a mesh axis runs over, the one named last changes fastest.
Arguments:
- concentration: float32 [128, 256, 256], P('tx', 'ty'), may hold values from -6 to 6
- source: float32 [128, 256, 256], P('tx', 'ty'), may hold values from -4 to 4
- material: int32 [128, 256, 256], P('tx', 'ty'), may hold values from 0 to 7
Outputs:
- updated: float32 [128, 256, 256], P('tx', 'ty')
All inputs are finite; a program needn't handle non-finite values.
Results may differ from a plain program's by a relative error of at most 0.00017.
Values sent between devices are 32-bit elements; how exact they have to be, the bound alone decides.
A program may use at most 128 MiB of HBM per device.

v0:
```python
import jax
import jax.numpy as jnp
from jax import lax
from jax.experimental import pallas as pl
from jax.experimental.pallas import tpu as pltpu
from jax.sharding import PartitionSpec as P

MESH = pl.DeviceIdType.MESH
F32 = jnp.float32
BF16 = jnp.bfloat16
RATE = 0.001
RELAX = 0.8
TABLE = (0.15, 0.3, 0.5, 0.8, 1.2, 2.0, 3.2, 5.0)
N = 16


def iota(shape, axis):
    return lax.broadcasted_iota(jnp.int32, shape, axis)


def roll(v, shift, axis):
    return pltpu.roll(v, shift % v.shape[axis], axis)


def dot01(v, m):
    hi = v.astype(BF16)
    rest = v - hi.astype(F32)
    mid = rest.astype(BF16)
    low = (rest - mid.astype(F32)).astype(BF16)
    a, b, c = [jnp.dot(piece, m, preferred_element_type=F32) for piece in (hi, mid, low)]
    return a + (b + c)


def each(low, high, unroll, body):
    count = high - low
    whole = count // unroll
    if whole > 1:

        def step(i, carry):
            for k in range(unroll):
                body(low + i * unroll + k)
            return carry

        lax.fori_loop(0, whole, step, 0)
        rest = low + whole * unroll
    else:
        rest = low
    for x in range(rest, high):
        body(x)


def make_ops(kappa, ops, scale, layers, unroll):
    cx, cy, cz, w = ops
    half = 0.5 * scale

    def couple(x):
        k = kappa[x]
        cx[x] = half * (k + kappa[x + 1])
        cy[x] = half * (k + roll(k, -1, 0))
        cz[x] = half * (k + roll(k, -1, 1))

    def weigh(x):
        a, b = cy[x], cz[x]
        diag = (RATE + cx[x] + cx[x - 1]) + (a + roll(a, 1, 0)) + (b + roll(b, 1, 1))
        w[x] = RELAX / diag

    each(0, layers - 1, unroll, couple)
    each(1, layers - 1, unroll, weigh)


def residual(v, below, above, g, cx, cxm, cy, cz):
    fy = cy * (roll(v, -1, 0) - v)
    fz = cz * (roll(v, -1, 1) - v)
    r = (g - RATE * v) + (cx * (above - v) - cxm * (v - below))
    return r + (fy - roll(fy, 1, 0)) + (fz - roll(fz, 1, 1))


def res_at(v, g, ops, x):
    cx, cy, cz, _ = ops
    return residual(v[x], v[x - 1], v[x + 1], g[x], cx[x], cx[x - 1], cy[x], cz[x])


def sweep(v, out, g, ops, low, high, unroll):
    def body(x):
        out[x] = v[x] + ops[3][x] * res_at(v, g, ops, x)

    each(low, high, unroll, body)


def x_hi_next(v):
    lane = iota(v.shape, 1)
    return jnp.where(lane % 4 == 3, roll(v, 3, 1), roll(v, -1, 1))


def x_hi_prev(v):
    lane = iota(v.shape, 1)
    return jnp.where(lane % 4 == 0, roll(v, -3, 1), roll(v, 1, 1))


def low_couple(kappa, s, scale):
    half = 0.5 * scale
    nxt = kappa[1:] + [x_hi_next(kappa[0])]
    cx = [half * (k + n) for k, n in zip(kappa, nxt)]
    cy = [half * (k + roll(k, -s, 0)) for k in kappa]
    cz = [half * (k + roll(k, -4 * s, 1)) for k in kappa]
    cxm = [x_hi_prev(cx[-1])] + cx[:-1]
    w = []
    for a, am, b, c in zip(cx, cxm, cy, cz):
        diag = (RATE + a + am) + (b + roll(b, s, 0)) + (c + roll(c, 4 * s, 1))
        w.append(RELAX / diag)
    return cx, cy, cz, w


def low_res(v, g, ops, s):
    cx, cy, cz, _ = ops
    nxt = v[1:] + [x_hi_next(v[0])]
    fx = [c * (n - u) for c, n, u in zip(cx, nxt, v)]
    fxm = [x_hi_prev(fx[-1])] + fx[:-1]
    out = []
    for u, f, a, am, b, c in zip(v, g, fx, fxm, cy, cz):
        fy = b * (roll(u, -s, 0) - u)
        fz = c * (roll(u, -4 * s, 1) - u)
        r = (f - RATE * u) + (a - am)
        out.append(r + (fy - roll(fy, s, 0)) + (fz - roll(fz, 4 * s, 1)))
    return out


def low_sweep(v, g, ops, s):
    return [u + w * r for u, w, r in zip(v, ops[3], low_res(v, g, ops, s))]


def low_restrict(v, s):
    if len(v) > 1:
        v = [v[2 * k] + v[2 * k + 1] for k in range(len(v) // 2)]
    else:
        u = v[0]
        lane = iota(u.shape, 1)
        v = [u + jnp.where(lane % 2 == 0, roll(u, -1, 1), roll(u, 1, 1))]
    out = []
    for u in v:
        row, lane = iota(u.shape, 0), iota(u.shape, 1)
        u = u + jnp.where((row // s) % 2 == 0, roll(u, -s, 0), roll(u, s, 0))
        u = u + jnp.where((lane // (4 * s)) % 2 == 0, roll(u, -4 * s, 1), roll(u, 4 * s, 1))
        out.append(u * 0.125)
    return out


def pack_six(v):
    lane = iota((8, 128), 1)
    y = (lane % 32) // 4
    out = v[24:32]
    for k in (2, 1, 0):
        out = jnp.where(y == k, v[8 * k : 8 * k + 8], out)
    return out


def kernel(conc, source, material, out, *scratch):
    names = [name for name, _ in SCRATCH]
    s = dict(zip(names, scratch))
    ops0, ops1, ops2 = [[s[f"{name}{level}"] for name in ("cx", "cy", "cz", "w")] for level in (0, 1, 2)]
    me_x, me_y = lax.axis_index("tx"), lax.axis_index("ty")

    def device(dx, dy):
        return (lax.rem(me_x + (dx + N), N), lax.rem(me_y + (dy + N), N))

    counter = {}

    def copy(group, src, dst, dx, dy):
        k = counter.get(group, 0)
        counter[group] = k + 1
        c = pltpu.make_async_remote_copy(
            src, dst, s[group + "_s"].at[k], s[group + "_r"].at[k], device_id=device(dx, dy), device_id_type=MESH
        )
        c.start()
        return c

    sent = []

    def arrive(copies):
        for c in copies:
            c.wait_recv()
        sent.extend(copies)

    tile0 = (slice(3, 11), slice(0, 16))
    loads = [
        pltpu.make_async_copy(material, s["mat"], s["load"].at[0]),
        pltpu.make_async_copy(conc, s["va"].at[3:11, 0:16], s["load"].at[1]),
        pltpu.make_async_copy(source, s["src"].at[3:11, 0:16], s["load"].at[2]),
    ]
    for c in loads:
        c.start()
    barrier = pltpu.get_barrier_semaphore()
    peers = [(d, 0) for d in range(1, N)] + [(0, d) for d in range(1, N)]
    peers += [(a, b) for a in (-2, -1, 1, 2) for b in (-1, 1)]
    for p in peers:
        pl.semaphore_signal(barrier, inc=1, device_id=device(*p), device_id_type=MESH)

    def matrix(name, rule):
        shape = s[name].shape
        s[name][...] = jnp.where(rule(iota(shape, 0), iota(shape, 1)), 1.0, 0.0).astype(BF16)

    matrix("r01", lambda i, j: i // 2 == j)
    matrix("r12", lambda i, j: i // 2 == j % 64)
    matrix("r23", lambda i, j: i // 2 == j // 4)
    matrix("p32", lambda i, j: i // 4 == (j % 64) // 2)
    matrix("p21", lambda i, j: i == j // 2)
    matrix("p10", lambda i, j: i == j // 2)
    matrix("sel", lambda i, j: ((i % 32) // 4 < 4) & (i % 2 == 0) & (j == ((i % 32) // 4) * 8 + (i // 32) * 2 + (i % 4) // 2))
    matrix("spr", lambda i, j: i == (j // 128) * 8 + ((j % 128) // 32) * 2 + (j % 4) // 2)

    loads[0].wait()
    k0 = s["k0"]

    def lookup(x):
        m = s["mat"][x]
        result = jnp.zeros(m.shape, F32)
        for slot, value in enumerate(TABLE):
            result = jnp.where(m == slot, F32(value), result)
        k0[x + 3, 0:16] = result

    each(0, 8, 2, lookup)
    loads[1].wait()
    loads[2].wait()
    pl.semaphore_wait(barrier, len(peers))

    def halo0(group, ref, dest, w, c):
        edge, below = s[group + "_e"], s[group + "_b"]
        for x in range(8):
            edge[x] = roll(ref[x + 3, 8:16], w, 0)
        copies = []
        for dx, dy in ((1, 0), (-1, 0), (0, 1), (0, -1), (1, 1), (1, -1), (-1, 1), (-1, -1)):
            n = c if dy else w
            x0, x1 = {0: (3, 11), -1: (3, 3 + n), 1: (11 - n, 11)}[dx]
            y0, y1 = x0 - 8 * dx, x1 - 8 * dx
            if dy == 0:
                copies.append(copy(group, ref.at[x0:x1, 0:16], dest.at[y0:y1, 0:16], dx, dy))
            elif dy < 0:
                copies.append(copy(group, ref.at[x0:x1, 0:w], dest.at[y0:y1, 16 : 16 + w], dx, dy))
            else:
                copies.append(copy(group, edge.at[x0 - 3 : x1 - 3, 0:w], below.at[y0:y1, 0:w], dx, dy))
        return copies

    def merge0(group, dest, w):
        below = s[group + "_b"]
        row = iota((8, 256), 0)
        for x in range(14):
            dest[x, 16:24] = jnp.where(row < 4, dest[x, 16:24], roll(below[x], -w, 0))

    in_k0 = halo0("hk", k0, k0, 3, 2)
    in_va = halo0("hv", s["va"], s["va"], 3, 2)
    in_src = halo0("hs", s["src"], s["src"], 2, 1)

    t0, t1, t2 = s["t0"], s["t1"], s["t2"]

    def put0(c, pair):
        t0[c, 0] = pair[:16, :128]
        t0[c, 1] = pair[:16, 128:]

    def take0():
        rows = []
        for c in range(4):
            halves = [t0[c, h, pl.ds(0, 8, stride=2), :] + t0[c, h, pl.ds(1, 8, stride=2), :] for h in range(2)]
            rows.append(jnp.concatenate(halves, axis=1))
        return dot01(jnp.concatenate(rows, axis=0), s["r01"][...]) * 0.125

    def row_pairs(ref, k, start, count):
        return ref[k, pl.ds(start, count, stride=2), :] + ref[k, pl.ds(start + 1, count, stride=2), :]

    k1, k2, x2k, x2f = s["k1"], s["k2"], s["x2k"], s["x2f"]
    for c in range(4):
        put0(c, k0[3 + 2 * c, 0:16] + k0[4 + 2 * c, 0:16])
    tile = take0()
    for c in range(4):
        k1[7 + c, 0:8] = tile[8 * c : 8 * c + 8]

    def halo1(group, ref, w):
        copies = []
        for dx, dy in ((1, 0), (-1, 0), (0, 1), (0, -1), (2, 0), (-2, 0), (1, 1), (1, -1), (-1, 1), (-1, -1), (2, 1), (2, -1), (-2, 1), (-2, -1)):
            nx = {0: 4, 1: 4, 2: w - 4 if dy == 0 else w - 5}[abs(dx)]
            ny = 8 if dy == 0 else {0: w, 1: w - 1, 2: w - 5}[abs(dx)]
            xs = slice(11 - nx, 11) if dx > 0 else slice(7, 7 + nx)
            xd = slice(xs.start - 4 * dx, xs.stop - 4 * dx)
            ys = slice(0, 8) if dy > 0 else slice(0, ny)
            yd = slice(16, 24) if dy > 0 else slice(-8 * dy, ny - 8 * dy)
            copies.append(copy(group, ref.at[xs, ys], ref.at[xd, yd], dx, dy))
        return copies

    in_k1 = halo1("h1k", k1, 7)

    def to_level2(get):
        parts = []
        for c in range(len(get) // 2):
            pair = get[2 * c] + get[2 * c + 1]
            if len(pair) == 8:
                t1[c, 4:12] = pair
            else:
                t1[c] = roll(pair, 4, 0)
        for c in range(len(get) // 2):
            parts.append(row_pairs(t1, c, 0, 8))
        return dot01(jnp.concatenate(parts, axis=0), s["r12"][...]) * 0.125

    def to_level3(pair, row0):
        t2[0] = dot01(pair, s["r23"][...]) * 0.125
        return row_pairs(t2, 0, row0, 2)

    low = to_level2([tile[8 * c : 8 * c + 8] for c in range(4)])
    for c in range(2):
        x2k[6 + c, 2] = low[8 * c + 2 : 8 * c + 6]
    base = to_level3(low[0:8] + low[8:16], 2)

    def ring_x(group, ref, tile_ref, value):
        tile_ref[...] = value
        ref[me_x] = value
        return [copy(group, tile_ref, ref.at[me_x], d, 0) for d in range(1, N)]

    def window_x(group, ref):
        return [
            copy(group, ref.at[6:8, 2], ref.at[6 - 2 * d : 8 - 2 * d, 2], d, 0) for d in (1, -1, 2, -2, 3, -3)
        ]

    def slab(ref):
        lane = iota((2, 128), 1)
        out_parts = []
        for k in range(4):
            v = ref[12 + k]
            for h in (2, 1, 0):
                v = jnp.where(lane % 4 == h, ref[4 * h + k], v)
            out_parts.append(v)
        return out_parts

    def ring_y(group, ref, slab_ref, parts):
        for k in range(4):
            slab_ref[k] = parts[k]
            ref[k, me_y] = parts[k]
        return [copy(group, slab_ref, ref.at[:, me_y], 0, d) for d in range(1, N)]

    def window_y(group, ref):
        return [copy(group, ref.at[:, 2], ref.at[:, 2 - d], 0, d) for d in (1, -1, 2, -2)]

    def window(ref, dest):
        for x in range(14):
            dest[x] = ref[x].reshape(20, 128)[2:18]

    in_ka = ring_x("ka", s["ka"], s["kt"], base)
    in_k2a = window_x("k2a", x2k)

    arrive(in_k0)
    merge0("hk", k0, 3)
    make_ops(k0, ops0, 1.0, 14, 3)
    arrive(in_va)
    arrive(in_src)
    merge0("hv", s["va"], 3)
    merge0("hs", s["src"], 2)
    va, vb, vc, vd, ve, src, g0 = [s[name] for name in ("va", "vb", "vc", "vd", "ve", "src", "g0")]

    def force(x):
        g0[x] = RATE * va[x] + src[x]

    each(1, 13, 3, force)
    sweep(va, vb, g0, ops0, 1, 13, 3)
    sweep(vb, vc, g0, ops0, 2, 12, 2)

    def down0(c):
        put0(c, res_at(vc, g0, ops0, 2 * c + 3) + res_at(vc, g0, ops0, 2 * c + 4))

    each(0, 4, 1, down0)
    tile = take0()
    f1 = s["f1"]
    for c in range(4):
        f1[7 + c, 0:8] = tile[8 * c : 8 * c + 8]
    in_f1 = halo1("h1f", f1, 6)

    arrive(in_ka)
    in_kb = ring_y("kb", s["kb"], s["ks"], slab(s["ka"]))
    arrive(in_k2a)
    in_k2b = window_y("k2b", x2k)
    stay = pltpu.make_async_copy(vc.at[tile0], vd.at[tile0], s["load"].at[0])
    stay.start()
    in_vd = halo0("hd", vc, vd, 2, 1)

    arrive(in_k1)
    make_ops(k1, ops1, 0.25, 18, 4)
    arrive(in_f1)

    v1a, v1b = s["v1a"], s["v1b"]

    def start1(x):
        v1a[x] = ops1[3][x] * f1[x]

    each(1, 17, 4, start1)
    sweep(v1a, v1b, f1, ops1, 2, 16, 7)
    low = to_level2([res_at(v1b, f1, ops1, x) for x in range(3, 15)])
    f2l = s["f2l"]
    f2 = s["f2"]
    for c in range(6):
        f2l[c] = low[8 * c : 8 * c + 8]
    for c in range(2):
        x2f[6 + c, 2] = low[8 * c + 18 : 8 * c + 22]

    arrive(in_k2b)
    window(x2k, k2)
    make_ops(k2, ops2, 0.0625, 14, 13)
    v2a, v2b = s["v2a"], s["v2b"]
    near = [[ref[x, 4:12] for x in range(4, 10)] for ref in ops2]
    fl = [f2l[c] for c in range(6)]
    vl = [near[3][c] * fl[c] for c in range(6)]

    def res_near(v, c):
        return residual(v[c], v[c - 1], v[c + 1], fl[c], near[0][c], near[0][c - 1], near[1][c], near[2][c])

    ul = [None] + [vl[c] + near[3][c] * res_near(vl, c) for c in range(1, 5)]
    base = to_level3(res_near(ul + [None], 2) + res_near(ul + [None], 3), 2)
    in_fa = ring_x("fa", s["fa"], s["ft"], base)
    in_f2a = window_x("f2a", x2f)

    arrive(in_kb)
    kap3 = [s["kb"][k].reshape(32, 128) for k in range(4)]
    kap4 = low_restrict(kap3, 1)
    kap5 = low_restrict(kap4, 2)
    kap6 = low_restrict(kap5, 4)[0]
    for level, kap, spread in ((3, kap3, 1), (4, kap4, 2), (5, kap5, 4)):
        made = low_couple(kap, spread, 1.0 / 4.0**level)
        for number in range(4):
            for k in range(len(kap)):
                s[f"low{level}"][number, k] = made[number][k]

    krow = dot01(pack_six(kap6), s["sel"][...])[0:1]
    q, p = iota((32, 128), 0), iota((32, 128), 1)
    kcol = jnp.sum(jnp.where(q == p, krow, 0.0), axis=1, keepdims=True)
    dy, dz, same_x = (q // 8 - p // 8 + 4) % 4, ((q % 8) // 2 - (p % 8) // 2 + 4) % 4, q % 2 == p % 2
    links = jnp.where(same_x & (dz == 0) & (dy % 2 == 1), 1.0, 0.0) + jnp.where(same_x & (dy == 0) & (dz % 2 == 1), 1.0, 0.0)
    links = links + jnp.where((dz == 0) & (dy == 0) & (q % 2 != p % 2), 2.0, 0.0)
    links = jnp.where(p < 32, links, 0.0)
    off = (0.5 / 4096.0) * links * (krow + kcol)
    diag = RATE + jnp.sum(off, axis=1, keepdims=True)
    m_ref = s["m6"]
    m_ref[...] = jnp.where(q == p, diag, jnp.where(p == q + 32, 1.0, -off))

    def eliminate(k, carry):
        m = m_ref[...]
        pivot_row = m_ref[pl.ds(k, 1), :]
        column = jnp.sum(jnp.where(p == k, m, 0.0), axis=1, keepdims=True)
        pivot = jnp.sum(jnp.where(iota((1, 128), 1) == k, pivot_row, 0.0), axis=1, keepdims=True)
        scaled = pivot_row / pivot
        m_ref[...] = jnp.where(q == k, scaled, m - column * scaled)
        return carry

    lax.fori_loop(0, 16, eliminate, 0)

    arrive(in_fa)
    in_fb = ring_y("fb", s["fb"], s["fs"], slab(s["fa"]))
    arrive(in_f2a)
    in_f2b = window_y("f2b", x2f)
    lax.fori_loop(16, 32, eliminate, 0)
    inverse = roll(m_ref[...], -32, 1)
    inverse = jnp.concatenate([jnp.where(p < 32, inverse, 0.0), jnp.zeros((96, 128), F32)], axis=0)
    s["inv"][...] = inverse

    def low_ops(level, count):
        return [[s[f"low{level}"][number, k] for k in range(count)] for number in range(4)]

    arrive(in_fb)
    g3 = [s["fb"][k].reshape(32, 128) for k in range(4)]
    o3, o4, o5 = low_ops(3, 4), low_ops(4, 2), low_ops(5, 1)

    def down(g, o, spread):
        v = low_sweep([w * f for w, f in zip(o[3], g)], g, o, spread)
        return v, low_restrict(low_res(v, g, o, spread), spread)

    v3, g4 = down(g3, o3, 1)
    v4, g5 = down(g4, o4, 2)
    v5, g6 = down(g5, o5, 4)
    x6 = dot01(pack_six(g6[0]), s["sel"][...])
    x6 = jnp.dot(x6, s["inv"][...], precision=lax.Precision.HIGHEST, preferred_element_type=F32)
    x6 = dot01(x6, s["spr"][...])
    x6 = jnp.concatenate([x6[:, 128 * k : 128 * k + 128] for k in range(4)], axis=0)

    def up(v, e, g, o, spread):
        v = [u + e[k * len(e) // len(v)] for k, u in enumerate(v)]
        return low_sweep(low_sweep(v, g, o, spread), g, o, spread)

    v5 = up(v5, [x6], g5, o5, 4)
    v4 = up(v4, v5, g4, o4, 2)
    v3 = up(v3, v4, g3, o3, 1)

    e3, e2, e1 = s["e3"], s["e2"], s["e1"]
    turn = lax.rem(2 * N - 2 * me_y + 3, 2 * N)
    for k in range(4):
        e3[k] = pltpu.roll(v3[k], turn, 0)[0:8]
    picks = []
    lane8 = iota((8, 128), 1)
    for d in range(-2, 3):
        x = lax.rem(me_x + (d + N), N)
        picks.append(jnp.where(lane8 % 4 == x // 4, e3[lax.rem(x, 4)], 0.0))
    spread3 = dot01(jnp.concatenate(picks, axis=0), s["p32"][...])
    for c in range(5):
        e2[c + 1, pl.ds(0, 8, stride=2), :] = spread3[8 * c : 8 * c + 8]
        e2[c + 1, pl.ds(1, 8, stride=2), :] = spread3[8 * c : 8 * c + 8]

    arrive(in_f2b)
    window(x2f, f2)
    for x in range(1, 13):
        v2a[x] = ops2[3][x] * f2[x]
    sweep(v2a, v2b, f2, ops2, 2, 12, 10)
    for x in range(2, 12):
        v2b[x] = v2b[x] + e2[x // 2]
    sweep(v2b, v2a, f2, ops2, 3, 11, 8)
    sweep(v2a, v2b, f2, ops2, 4, 10, 6)

    spread2 = dot01(jnp.concatenate([v2b[x] for x in range(4, 10)], axis=0), s["p21"][...])
    for c in range(6):
        e1[c, pl.ds(0, 16, stride=2), :] = spread2[16 * c : 16 * c + 16]
        e1[c, pl.ds(1, 16, stride=2), :] = spread2[16 * c : 16 * c + 16]
    for x in range(4, 14):
        c = (x + 5) // 2 - 4
        v1b[x] = v1b[x] + jnp.concatenate([e1[c, 12:28], e1[c, 4:12]], axis=0)
    sweep(v1b, v1a, f1, ops1, 5, 13, 8)
    sweep(v1a, v1b, f1, ops1, 6, 12, 6)

    e0 = s["e0"]
    for c in range(6):
        e0[c, pl.ds(0, 24, stride=2), :] = v1b[6 + c]
        e0[c, pl.ds(1, 24, stride=2), :] = v1b[6 + c]
    row8 = iota((8, 128), 0)
    parts = []
    for c in range(6):
        parts += [e0[c, 0:16], jnp.where(row8 < 4, e0[c, 16:24], e0[c, 40:48])]
    spread1 = dot01(jnp.concatenate(parts, axis=0), s["p10"][...])
    stay.wait()
    arrive(in_vd)
    merge0("hd", vd, 2)
    for x in range(1, 13):
        c = (x + 11) // 2 - 6
        ve[x] = vd[x] + spread1[24 * c : 24 * c + 24]
    sweep(ve, vb, g0, ops0, 2, 12, 2)

    def last(x):
        v = vb[x + 3] + ops0[3][x + 3] * res_at(vb, g0, ops0, x + 3)
        out[x] = v[0:16]

    each(0, 8, 2, last)
    for c in sent:
        c.wait_send()


def scratch_list():
    def vmem(*shape, kind=F32):
        return pltpu.VMEM(shape, kind)

    made = [("mat", vmem(8, 16, 256, kind=jnp.int32))]
    for name in ("k0", "va", "vb", "vc", "vd", "ve", "src", "g0", "cx0", "cy0", "cz0", "w0"):
        made.append((name, vmem(14, 24, 256)))
    for name in ("k1", "f1", "v1a", "v1b", "cx1", "cy1", "cz1", "w1"):
        made.append((name, vmem(18, 24, 128)))
    for name in ("k2", "f2", "v2a", "v2b", "cx2", "cy2", "cz2", "w2"):
        made.append((name, vmem(14, 16, 128)))
    for name in ("x2k", "x2f"):
        made.append((name, vmem(14, 5, 4, 128)))
    for name in ("hk", "hv", "hs", "hd"):
        made.append((name + "_e", vmem(8, 8, 256)))
        made.append((name + "_b", vmem(14, 8, 256)))
    made.append(("f2l", vmem(6, 8, 128)))
    for name in ("ka", "fa"):
        made.append((name, vmem(N, 2, 128)))
    for name in ("kb", "fb"):
        made.append((name, vmem(4, N, 2, 128)))
    for name in ("kt", "ft"):
        made.append((name, vmem(2, 128)))
    for name in ("ks", "fs"):
        made.append((name, vmem(4, 2, 128)))
    made.append(("t0", vmem(4, 2, 16, 128)))
    made.append(("t1", vmem(6, 24, 128)))
    made.append(("t2", vmem(1, 8, 128)))
    made.append(("e3", vmem(4, 8, 128)))
    made.append(("e2", vmem(7, 16, 128)))
    made.append(("e1", vmem(6, 32, 128)))
    made.append(("e0", vmem(6, 48, 128)))
    made.append(("low3", vmem(4, 4, 32, 128)))
    made.append(("low4", vmem(4, 2, 32, 128)))
    made.append(("low5", vmem(4, 1, 32, 128)))
    made.append(("m6", vmem(32, 128)))
    made.append(("inv", vmem(128, 128)))
    for name, shape in (("r01", (256, 128)), ("r12", (128, 128)), ("r23", (128, 128)), ("p32", (128, 128)), ("p21", (128, 128)), ("p10", (128, 256)), ("sel", (128, 128)), ("spr", (128, 512))):
        made.append((name, vmem(*shape, kind=BF16)))
    made.append(("load", pltpu.SemaphoreType.DMA((3,))))
    groups = {"hk": 8, "hv": 8, "hs": 8, "hd": 8, "h1k": 14, "h1f": 14, "ka": 15, "kb": 15, "fa": 15, "fb": 15, "k2a": 6, "f2a": 6, "k2b": 4, "f2b": 4}
    for name, count in groups.items():
        made.append((name + "_s", pltpu.SemaphoreType.DMA((count,))))
        made.append((name + "_r", pltpu.SemaphoreType.DMA((count,))))
    return made


SCRATCH = scratch_list()


def shards(concentration, source, material):
    return pl.pallas_call(
        kernel,
        out_shape=jax.ShapeDtypeStruct(concentration.shape, F32),
        in_specs=[pl.BlockSpec(memory_space=pltpu.HBM)] * 3,
        out_specs=pl.BlockSpec(memory_space=pltpu.VMEM),
        scratch_shapes=[shape for _, shape in SCRATCH],
        compiler_params=pltpu.CompilerParams(collective_id=0, has_side_effects=True, vmem_limit_bytes=48 << 20),
        cost_estimate=pl.CostEstimate(flops=20_000_000, bytes_accessed=1_000_000, transcendentals=0),
        name="vcycle",
    )(concentration, source, material)


def solution(mesh):
    placed = P("tx", "ty", None)
    return jax.shard_map(shards, mesh=mesh, in_specs=(placed,) * 3, out_specs=placed, check_vma=False)
```

profile of v0, /device:TPU:1, one launch (start us, length us, event | category | flops | bytes accessed | tf_op | source)
XLA Modules:
  0.0 49.7 jit_solution(8106175084256310938)
XLA Ops:
  0.0 0.0 copy-start
  0.0 0.9 %copy-done = f32[8,16,256]{2,1,0:T(8,128)S(1)} copy-done((f32[8,16,256]{2,1,0:T(8,128)S(1)}, f32[8,16,256]{2,1,0:T(8,128)}, u32[]{:S(2)}) %copy-start) | copy-done | bytes 131096
  0.9 0.0 copy-start.1
  0.9 0.9 %copy-done.1 = f32[8,16,256]{2,1,0:T(8,128)S(1)} copy-done((f32[8,16,256]{2,1,0:T(8,128)S(1)}, f32[8,16,256]{2,1,0:T(8,128)}, u32[]{:S(2)}) %copy-start.1) | copy-done | bytes 131096
  1.8 0.0 copy-start.2
  1.8 0.9 %copy-done.2 = s32[8,16,256]{2,1,0:T(8,128)S(1)} copy-done((s32[8,16,256]{2,1,0:T(8,128)S(1)}, s32[8,16,256]{2,1,0:T(8,128)}, u32[]{:S(2)}) %copy-start.2) | copy-done | bytes 131096
  2.7 46.3 %vcycle.1 = f32[8,16,256]{2,1,0:T(8,128)S(1)} custom-call(f32[8,16,256]{2,1,0:T(8,128)S(1)} %copy-done, f32[8,16,256]{2,1,0:T(8,128)S(1)} %copy-done.1, s32[8,16,256]{2,1,0:T(8,128)S(1)} %copy-done.2), custom_call_target="tpu_custom_call" | custom-call | flops 20000000 | bytes 1000000 | tf_op jit(solution)/shard_map/vcycle/pallas_call | solution.py:597
  49.1 0.7 %copy.5 = f32[8,16,256]{2,1,0:T(8,128)} copy(f32[8,16,256]{2,1,0:T(8,128)S(1)} %vcycle.1) | data formatting | bytes 262144
Async XLA Ops:
  0.0 0.9 %copy-start = (f32[8,16,256]{2,1,0:T(8,128)S(1)}, f32[8,16,256]{2,1,0:T(8,128)}, u32[]{:S(2)}) copy-start(f32[8,16,256]{2,1,0:T(8,128)} %conc.1) | copy-start | bytes 393220
  0.9 0.9 %copy-start.1 = (f32[8,16,256]{2,1,0:T(8,128)S(1)}, f32[8,16,256]{2,1,0:T(8,128)}, u32[]{:S(2)}) copy-start(f32[8,16,256]{2,1,0:T(8,128)} %source.1) | copy-start | bytes 393220
  1.8 0.9 %copy-start.2 = (s32[8,16,256]{2,1,0:T(8,128)S(1)}, s32[8,16,256]{2,1,0:T(8,128)}, u32[]{:S(2)}) copy-start(s32[8,16,256]{2,1,0:T(8,128)} %material.1) | copy-start | bytes 393220
where the time goes:
time: 49.9 us; the launch traced here: 49.7 us
  Pallas kernels  46.3 us (93%)
  local copies, waits for them, and re-layouts  3.37 us (7%)
    pallas_call x1, Pallas kernels, shards(): pl.pallas_call(kernel, out_shape=jax.ShapeDtypeStruct(concentration.shape...  46.3 us
    unnamed x7, local copies, waits for them, and re-layouts  3.37 us

commit v1 on v0

--- a/solution.py
+++ b/solution.py
@@ -24,11 +24,12 @@
 
 def dot01(v, m):
     hi = v.astype(BF16)
-    rest = v - hi.astype(F32)
-    mid = rest.astype(BF16)
-    low = (rest - mid.astype(F32)).astype(BF16)
-    a, b, c = [jnp.dot(piece, m, preferred_element_type=F32) for piece in (hi, mid, low)]
-    return a + (b + c)
+    low = (v - hi.astype(F32)).astype(BF16)
+    rows = len(v)
+    if rows % 16 == 0:
+        both = jnp.dot(jnp.concatenate([hi, low], axis=0), m, preferred_element_type=F32)
+        return both[:rows] + both[rows:]
+    return jnp.dot(hi, m, preferred_element_type=F32) + jnp.dot(low, m, preferred_element_type=F32)
 
 
 def each(low, high, unroll, body):
@@ -192,6 +193,7 @@
     barrier = pltpu.get_barrier_semaphore()
     peers = [(d, 0) for d in range(1, N)] + [(0, d) for d in range(1, N)]
     peers += [(a, b) for a in (-2, -1, 1, 2) for b in (-1, 1)]
+    peers.sort(key=lambda p: -min(p[0] % N, -p[0] % N) - min(p[1] % N, -p[1] % N))
     for p in peers:
         pl.semaphore_signal(barrier, inc=1, device_id=device(*p), device_id_type=MESH)
 
@@ -285,8 +287,6 @@
             copies.append(copy(group, ref.at[xs, ys], ref.at[xd, yd], dx, dy))
         return copies
 
-    in_k1 = halo1("h1k", k1, 7)
-
     def to_level2(get):
         parts = []
         for c in range(len(get) // 2):
@@ -341,9 +341,9 @@
         for x in range(14):
             dest[x] = ref[x].reshape(20, 128)[2:18]
 
+    in_k1 = halo1("h1k", k1, 7)
     in_ka = ring_x("ka", s["ka"], s["kt"], base)
     in_k2a = window_x("k2a", x2k)
-
     arrive(in_k0)
     merge0("hk", k0, 3)
     make_ops(k0, ops0, 1.0, 14, 3)
@@ -454,7 +454,13 @@
     lax.fori_loop(16, 32, eliminate, 0)
     inverse = roll(m_ref[...], -32, 1)
     inverse = jnp.concatenate([jnp.where(p < 32, inverse, 0.0), jnp.zeros((96, 128), F32)], axis=0)
-    s["inv"][...] = inverse
+    inverse = dot01(inverse, s["spr"][...])
+    hi = inverse.astype(BF16)
+    rest = inverse - hi.astype(F32)
+    mid = rest.astype(BF16)
+    pieces = (hi, mid, (rest - mid.astype(F32)).astype(BF16))
+    a, b, c = [jnp.dot(s["sel"][...], piece, preferred_element_type=F32) for piece in pieces]
+    s["inv"][...] = a + (b + c)
 
     def low_ops(level, count):
         return [[s[f"low{level}"][number, k] for k in range(count)] for number in range(4)]
@@ -470,9 +476,7 @@
     v3, g4 = down(g3, o3, 1)
     v4, g5 = down(g4, o4, 2)
     v5, g6 = down(g5, o5, 4)
-    x6 = dot01(pack_six(g6[0]), s["sel"][...])
-    x6 = jnp.dot(x6, s["inv"][...], precision=lax.Precision.HIGHEST, preferred_element_type=F32)
-    x6 = dot01(x6, s["spr"][...])
+    x6 = jnp.dot(pack_six(g6[0]), s["inv"][...], precision=lax.Precision.HIGHEST, preferred_element_type=F32)
     x6 = jnp.concatenate([x6[:, 128 * k : 128 * k + 128] for k in range(4)], axis=0)
 
     def up(v, e, g, o, spread):
@@ -579,7 +583,7 @@
     made.append(("low4", vmem(4, 2, 32, 128)))
     made.append(("low5", vmem(4, 1, 32, 128)))
     made.append(("m6", vmem(32, 128)))
-    made.append(("inv", vmem(128, 128)))
+    made.append(("inv", vmem(128, 512)))
     for name, shape in (("r01", (256, 128)), ("r12", (128, 128)), ("r23", (128, 128)), ("p32", (128, 128)), ("p21", (128, 128)), ("p10", (128, 256)), ("sel", (128, 128)), ("spr", (128, 512))):
         made.append((name, vmem(*shape, kind=BF16)))
     made.append(("load", pltpu.SemaphoreType.DMA((3,))))
@@ -600,7 +604,7 @@
         in_specs=[pl.BlockSpec(memory_space=pltpu.HBM)] * 3,
         out_specs=pl.BlockSpec(memory_space=pltpu.VMEM),
         scratch_shapes=[shape for _, shape in SCRATCH],
-        compiler_params=pltpu.CompilerParams(collective_id=0, has_side_effects=True, vmem_limit_bytes=48 << 20),
+        compiler_params=pltpu.CompilerParams(collective_id=0, has_side_effects=True, vmem_limit_bytes=56360960),
         cost_estimate=pl.CostEstimate(flops=20_000_000, bytes_accessed=1_000_000, transcendentals=0),
         name="vcycle",
     )(concentration, source, material)

time: 49.9 us -> 46.5 us (0.932)
  local copies, waits for them, and re-layouts: 3.37 us -> 0.66 us
  Pallas kernels: 46.3 us -> 45.7 us
    unnamed x7 -> x1, local copies, waits for them, and re-layouts: 3.37 us -> 0.66 us
    pallas_call x1, Pallas kernels: 46.3 us -> 45.7 us  [shards(): pl.pallas_call(kernel, out_shape=jax.ShapeDtypeStruct(concentration.shape...]
where the time goes in v1:
time: 46.5 us; the launch traced here: 46.4 us
  Pallas kernels  45.7 us (98%)
  local copies, waits for them, and re-layouts  0.66 us (1%)
    pallas_call x1, Pallas kernels, shards(): pl.pallas_call(kernel, out_shape=jax.ShapeDtypeStruct(concentration.shape...  45.7 us

profile of v1, /device:TPU:1, one launch (start us, length us, event | category | flops | bytes accessed | tf_op | source)
XLA Modules:
  0.0 46.4 jit_solution(446107923102142506)
XLA Ops:
  0.0 45.7 %vcycle.1 = f32[8,16,256]{2,1,0:T(8,128)S(1)} custom-call(f32[8,16,256]{2,1,0:T(8,128)} %conc.1, f32[8,16,256]{2,1,0:T(8,128)} %source.1, s32[8,16,256]{2,1,0:T(8,128)} %material.1), custom_call_target="tpu_custom_call" | custom-call | flops 20000000 | bytes 1000000 | tf_op jit(solution)/shard_map/vcycle/pallas_call | solution.py:601
  45.7 0.7 %copy.5 = f32[8,16,256]{2,1,0:T(8,128)} copy(f32[8,16,256]{2,1,0:T(8,128)S(1)} %vcycle.1) | data formatting | bytes 262144

commit v2 on v1

--- a/solution.py
+++ b/solution.py
@@ -220,7 +220,7 @@
             result = jnp.where(m == slot, F32(value), result)
         k0[x + 3, 0:16] = result
 
-    each(0, 8, 2, lookup)
+    each(0, 8, 8, lookup)
     loads[1].wait()
     loads[2].wait()
     pl.semaphore_wait(barrier, len(peers))
@@ -346,7 +346,7 @@
     in_k2a = window_x("k2a", x2k)
     arrive(in_k0)
     merge0("hk", k0, 3)
-    make_ops(k0, ops0, 1.0, 14, 3)
+    make_ops(k0, ops0, 1.0, 14, 13)
     arrive(in_va)
     arrive(in_src)
     merge0("hv", s["va"], 3)
@@ -356,14 +356,14 @@
     def force(x):
         g0[x] = RATE * va[x] + src[x]
 
-    each(1, 13, 3, force)
-    sweep(va, vb, g0, ops0, 1, 13, 3)
-    sweep(vb, vc, g0, ops0, 2, 12, 2)
+    each(1, 13, 12, force)
+    sweep(va, vb, g0, ops0, 1, 13, 12)
+    sweep(vb, vc, g0, ops0, 2, 12, 10)
 
     def down0(c):
         put0(c, res_at(vc, g0, ops0, 2 * c + 3) + res_at(vc, g0, ops0, 2 * c + 4))
 
-    each(0, 4, 1, down0)
+    each(0, 4, 4, down0)
     tile = take0()
     f1 = s["f1"]
     for c in range(4):
@@ -379,7 +379,7 @@
     in_vd = halo0("hd", vc, vd, 2, 1)
 
     arrive(in_k1)
-    make_ops(k1, ops1, 0.25, 18, 4)
+    make_ops(k1, ops1, 0.25, 18, 17)
     arrive(in_f1)
 
     v1a, v1b = s["v1a"], s["v1b"]
@@ -387,8 +387,8 @@
     def start1(x):
         v1a[x] = ops1[3][x] * f1[x]
 
-    each(1, 17, 4, start1)
-    sweep(v1a, v1b, f1, ops1, 2, 16, 7)
+    each(1, 17, 16, start1)
+    sweep(v1a, v1b, f1, ops1, 2, 16, 14)
     low = to_level2([res_at(v1b, f1, ops1, x) for x in range(3, 15)])
     f2l = s["f2l"]
     f2 = s["f2"]
@@ -536,13 +536,13 @@
     for x in range(1, 13):
         c = (x + 11) // 2 - 6
         ve[x] = vd[x] + spread1[24 * c : 24 * c + 24]
-    sweep(ve, vb, g0, ops0, 2, 12, 2)
+    sweep(ve, vb, g0, ops0, 2, 12, 10)
 
     def last(x):
         v = vb[x + 3] + ops0[3][x + 3] * res_at(vb, g0, ops0, x + 3)
         out[x] = v[0:16]
 
-    each(0, 8, 2, last)
+    each(0, 8, 8, last)
     for c in sent:
         c.wait_send()
 

time: 46.5 us -> 44.3 us (0.953)
  Pallas kernels: 45.7 us -> 43.6 us
    pallas_call x1, Pallas kernels: 45.7 us -> 43.6 us  [shards(): pl.pallas_call(kernel, out_shape=jax.ShapeDtypeStruct(concentration.shape...]
where the time goes in v2:
time: 44.3 us; the launch traced here: 44.2 us
  Pallas kernels  43.6 us (98%)
  local copies, waits for them, and re-layouts  0.66 us (1%)
    pallas_call x1, Pallas kernels, shards(): pl.pallas_call(kernel, out_shape=jax.ShapeDtypeStruct(concentration.shape...  43.6 us

profile of v2, /device:TPU:1, one launch (start us, length us, event | category | flops | bytes accessed | tf_op | source)
XLA Modules:
  0.0 44.2 jit_solution(4185108085093697891)
XLA Ops:
  0.0 43.6 %vcycle.1 = f32[8,16,256]{2,1,0:T(8,128)S(1)} custom-call(f32[8,16,256]{2,1,0:T(8,128)} %conc.1, f32[8,16,256]{2,1,0:T(8,128)} %source.1, s32[8,16,256]{2,1,0:T(8,128)} %material.1), custom_call_target="tpu_custom_call" | custom-call | flops 20000000 | bytes 1000000 | tf_op jit(solution)/shard_map/vcycle/pallas_call | solution.py:601
  43.6 0.7 %copy.5 = f32[8,16,256]{2,1,0:T(8,128)} copy(f32[8,16,256]{2,1,0:T(8,128)S(1)} %vcycle.1) | data formatting | bytes 262144

commit v3 on v2

--- a/solution.py
+++ b/solution.py
@@ -102,32 +102,31 @@
     half = 0.5 * scale
     nxt = kappa[1:] + [x_hi_next(kappa[0])]
     cx = [half * (k + n) for k, n in zip(kappa, nxt)]
-    cy = [half * (k + roll(k, -s, 0)) for k in kappa]
-    cz = [half * (k + roll(k, -4 * s, 1)) for k in kappa]
     cxm = [x_hi_prev(cx[-1])] + cx[:-1]
-    w = []
-    for a, am, b, c in zip(cx, cxm, cy, cz):
-        diag = (RATE + a + am) + (b + roll(b, s, 0)) + (c + roll(c, 4 * s, 1))
-        w.append(RELAX / diag)
-    return cx, cy, cz, w
-
-
-def low_res(v, g, ops, s):
-    cx, cy, cz, _ = ops
+    made = []
+    for k, a, am in zip(kappa, cx, cxm):
+        b, c = half * (k + roll(k, -s, 0)), half * (k + roll(k, -4 * s, 1))
+        bm, cm = roll(b, s, 0), roll(c, 4 * s, 1)
+        diag = (RATE + a + am) + (b + bm) + (c + cm)
+        w = RELAX / diag
+        made.append([w * a, w * am, w * b, w * bm, w * c, w * cm, w, diag * (1.0 / RELAX)])
+    return made
+
+
+def low_step(v, wg, ops, s):
     nxt = v[1:] + [x_hi_next(v[0])]
-    fx = [c * (n - u) for c, n, u in zip(cx, nxt, v)]
-    fxm = [x_hi_prev(fx[-1])] + fx[:-1]
+    prv = [x_hi_prev(v[-1])] + v[:-1]
     out = []
-    for u, f, a, am, b, c in zip(v, g, fx, fxm, cy, cz):
-        fy = b * (roll(u, -s, 0) - u)
-        fz = c * (roll(u, -4 * s, 1) - u)
-        r = (f - RATE * u) + (a - am)
-        out.append(r + (fy - roll(fy, s, 0)) + (fz - roll(fz, 4 * s, 1)))
+    for u, n, p, f, o in zip(v, nxt, prv, wg, ops):
+        along_x = o[0] * n + o[1] * p
+        along_y = o[2] * roll(u, -s, 0) + o[3] * roll(u, s, 0)
+        along_z = o[4] * roll(u, -4 * s, 1) + o[5] * roll(u, 4 * s, 1)
+        out.append((along_x + along_y) + (along_z + (f - RELAX * u)))
     return out
 
 
-def low_sweep(v, g, ops, s):
-    return [u + w * r for u, w, r in zip(v, ops[3], low_res(v, g, ops, s))]
+def low_sweep(v, wg, ops, s):
+    return [u + d for u, d in zip(v, low_step(v, wg, ops, s))]
 
 
 def low_restrict(v, s):
@@ -182,6 +181,11 @@
             c.wait_recv()
         sent.extend(copies)
 
+    def drain():
+        for c in sent:
+            c.wait_send()
+        sent.clear()
+
     tile0 = (slice(3, 11), slice(0, 16))
     loads = [
         pltpu.make_async_copy(material, s["mat"], s["load"].at[0]),
@@ -197,19 +201,6 @@
     for p in peers:
         pl.semaphore_signal(barrier, inc=1, device_id=device(*p), device_id_type=MESH)
 
-    def matrix(name, rule):
-        shape = s[name].shape
-        s[name][...] = jnp.where(rule(iota(shape, 0), iota(shape, 1)), 1.0, 0.0).astype(BF16)
-
-    matrix("r01", lambda i, j: i // 2 == j)
-    matrix("r12", lambda i, j: i // 2 == j % 64)
-    matrix("r23", lambda i, j: i // 2 == j // 4)
-    matrix("p32", lambda i, j: i // 4 == (j % 64) // 2)
-    matrix("p21", lambda i, j: i == j // 2)
-    matrix("p10", lambda i, j: i == j // 2)
-    matrix("sel", lambda i, j: ((i % 32) // 4 < 4) & (i % 2 == 0) & (j == ((i % 32) // 4) * 8 + (i // 32) * 2 + (i % 4) // 2))
-    matrix("spr", lambda i, j: i == (j // 128) * 8 + ((j % 128) // 32) * 2 + (j % 4) // 2)
-
     loads[0].wait()
     k0 = s["k0"]
 
@@ -223,12 +214,8 @@
     each(0, 8, 8, lookup)
     loads[1].wait()
     loads[2].wait()
-    pl.semaphore_wait(barrier, len(peers))
-
     def halo0(group, ref, dest, w, c):
         edge, below = s[group + "_e"], s[group + "_b"]
-        for x in range(8):
-            edge[x] = roll(ref[x + 3, 8:16], w, 0)
         copies = []
         for dx, dy in ((1, 0), (-1, 0), (0, 1), (0, -1), (1, 1), (1, -1), (-1, 1), (-1, -1)):
             n = c if dy else w
@@ -242,6 +229,15 @@
                 copies.append(copy(group, edge.at[x0 - 3 : x1 - 3, 0:w], below.at[y0:y1, 0:w], dx, dy))
         return copies
 
+    def edges0(group, ref, w):
+        for x in range(8):
+            s[group + "_e"][x] = roll(ref[x + 3, 8:16], w, 0)
+
+    edges0("hk", k0, 3)
+    edges0("hv", s["va"], 3)
+    edges0("hs", s["src"], 2)
+    pl.semaphore_wait(barrier, len(peers))
+
     def merge0(group, dest, w):
         below = s[group + "_b"]
         row = iota((8, 256), 0)
@@ -251,6 +247,19 @@
     in_k0 = halo0("hk", k0, k0, 3, 2)
     in_va = halo0("hv", s["va"], s["va"], 3, 2)
     in_src = halo0("hs", s["src"], s["src"], 2, 1)
+
+    def matrix(name, rule):
+        shape = s[name].shape
+        s[name][...] = jnp.where(rule(iota(shape, 0), iota(shape, 1)), 1.0, 0.0).astype(BF16)
+
+    matrix("r01", lambda i, j: i // 2 == j)
+    matrix("r12", lambda i, j: i // 2 == j % 64)
+    matrix("r23", lambda i, j: i // 2 == j // 4)
+    matrix("p32", lambda i, j: i // 4 == (j % 64) // 2)
+    matrix("p21", lambda i, j: i == j // 2)
+    matrix("p10", lambda i, j: i == j // 2)
+    matrix("sel", lambda i, j: ((i % 32) // 4 < 4) & (i % 2 == 0) & (j == ((i % 32) // 4) * 8 + (i // 32) * 2 + (i % 4) // 2))
+    matrix("spr", lambda i, j: i == (j // 128) * 8 + ((j % 128) // 32) * 2 + (j % 4) // 2)
 
     t0, t1, t2 = s["t0"], s["t1"], s["t2"]
 
@@ -277,7 +286,7 @@
 
     def halo1(group, ref, w):
         copies = []
-        for dx, dy in ((1, 0), (-1, 0), (0, 1), (0, -1), (2, 0), (-2, 0), (1, 1), (1, -1), (-1, 1), (-1, -1), (2, 1), (2, -1), (-2, 1), (-2, -1)):
+        for dx, dy in ((2, 1), (2, -1), (-2, 1), (-2, -1), (1, 1), (1, -1), (-1, 1), (-1, -1), (0, 1), (0, -1), (2, 0), (-2, 0), (1, 0), (-1, 0)):
             nx = {0: 4, 1: 4, 2: w - 4 if dy == 0 else w - 5}[abs(dx)]
             ny = 8 if dy == 0 else {0: w, 1: w - 1, 2: w - 5}[abs(dx)]
             xs = slice(11 - nx, 11) if dx > 0 else slice(7, 7 + nx)
@@ -370,12 +379,13 @@
         f1[7 + c, 0:8] = tile[8 * c : 8 * c + 8]
     in_f1 = halo1("h1f", f1, 6)
 
+    arrive(in_k2a)
+    in_k2b = window_y("k2b", x2k)
     arrive(in_ka)
     in_kb = ring_y("kb", s["kb"], s["ks"], slab(s["ka"]))
-    arrive(in_k2a)
-    in_k2b = window_y("k2b", x2k)
     stay = pltpu.make_async_copy(vc.at[tile0], vd.at[tile0], s["load"].at[0])
     stay.start()
+    edges0("hd", vc, 2)
     in_vd = halo0("hd", vc, vd, 2, 1)
 
     arrive(in_k1)
@@ -420,9 +430,9 @@
     kap6 = low_restrict(kap5, 4)[0]
     for level, kap, spread in ((3, kap3, 1), (4, kap4, 2), (5, kap5, 4)):
         made = low_couple(kap, spread, 1.0 / 4.0**level)
-        for number in range(4):
-            for k in range(len(kap)):
-                s[f"low{level}"][number, k] = made[number][k]
+        for k in range(len(kap)):
+            for number in range(8):
+                s[f"low{level}"][k, number] = made[k][number]
 
     krow = dot01(pack_six(kap6), s["sel"][...])[0:1]
     q, p = iota((32, 128), 0), iota((32, 128), 1)
@@ -460,32 +470,43 @@
     mid = rest.astype(BF16)
     pieces = (hi, mid, (rest - mid.astype(F32)).astype(BF16))
     a, b, c = [jnp.dot(s["sel"][...], piece, preferred_element_type=F32) for piece in pieces]
-    s["inv"][...] = a + (b + c)
+    inverse = a + (b + c)
+    hi = inverse.astype(BF16)
+    s["inv"][0] = hi
+    s["inv"][1] = (inverse - hi.astype(F32)).astype(BF16)
+
+    drain()
 
     def low_ops(level, count):
-        return [[s[f"low{level}"][number, k] for k in range(count)] for number in range(4)]
+        return [[s[f"low{level}"][k, number] for number in range(8)] for k in range(count)]
 
     arrive(in_fb)
     g3 = [s["fb"][k].reshape(32, 128) for k in range(4)]
     o3, o4, o5 = low_ops(3, 4), low_ops(4, 2), low_ops(5, 1)
 
     def down(g, o, spread):
-        v = low_sweep([w * f for w, f in zip(o[3], g)], g, o, spread)
-        return v, low_restrict(low_res(v, g, o, spread), spread)
-
-    v3, g4 = down(g3, o3, 1)
-    v4, g5 = down(g4, o4, 2)
-    v5, g6 = down(g5, o5, 4)
-    x6 = jnp.dot(pack_six(g6[0]), s["inv"][...], precision=lax.Precision.HIGHEST, preferred_element_type=F32)
+        wg = [q[6] * f for q, f in zip(o, g)]
+        v = low_sweep(wg, wg, o, spread)
+        step = low_step(v, wg, o, spread)
+        return v, wg, low_restrict([q[7] * d for q, d in zip(o, step)], spread)
+
+    v3, wg3, g4 = down(g3, o3, 1)
+    v4, wg4, g5 = down(g4, o4, 2)
+    v5, wg5, g6 = down(g5, o5, 4)
+    x6 = pack_six(g6[0])
+    hi = x6.astype(BF16).astype(F32)
+    both = jnp.concatenate([hi, x6 - hi], axis=0).astype(BF16)
+    large = jnp.dot(both, s["inv"][0], preferred_element_type=F32)
+    x6 = large[:8] + (large[8:] + jnp.dot(both, s["inv"][1], preferred_element_type=F32)[:8])
     x6 = jnp.concatenate([x6[:, 128 * k : 128 * k + 128] for k in range(4)], axis=0)
 
-    def up(v, e, g, o, spread):
+    def up(v, e, wg, o, spread):
         v = [u + e[k * len(e) // len(v)] for k, u in enumerate(v)]
-        return low_sweep(low_sweep(v, g, o, spread), g, o, spread)
-
-    v5 = up(v5, [x6], g5, o5, 4)
-    v4 = up(v4, v5, g4, o4, 2)
-    v3 = up(v3, v4, g3, o3, 1)
+        return low_sweep(low_sweep(v, wg, o, spread), wg, o, spread)
+
+    v5 = up(v5, [x6], wg5, o5, 4)
+    v4 = up(v4, v5, wg4, o4, 2)
+    v3 = up(v3, v4, wg3, o3, 1)
 
     e3, e2, e1 = s["e3"], s["e2"], s["e1"]
     turn = lax.rem(2 * N - 2 * me_y + 3, 2 * N)
@@ -543,8 +564,7 @@
         out[x] = v[0:16]
 
     each(0, 8, 8, last)
-    for c in sent:
-        c.wait_send()
+    drain()
 
 
 def scratch_list():
@@ -579,11 +599,11 @@
     made.append(("e2", vmem(7, 16, 128)))
     made.append(("e1", vmem(6, 32, 128)))
     made.append(("e0", vmem(6, 48, 128)))
-    made.append(("low3", vmem(4, 4, 32, 128)))
-    made.append(("low4", vmem(4, 2, 32, 128)))
-    made.append(("low5", vmem(4, 1, 32, 128)))
+    made.append(("low3", vmem(4, 8, 32, 128)))
+    made.append(("low4", vmem(2, 8, 32, 128)))
+    made.append(("low5", vmem(1, 8, 32, 128)))
     made.append(("m6", vmem(32, 128)))
-    made.append(("inv", vmem(128, 512)))
+    made.append(("inv", vmem(2, 128, 512, kind=BF16)))
     for name, shape in (("r01", (256, 128)), ("r12", (128, 128)), ("r23", (128, 128)), ("p32", (128, 128)), ("p21", (128, 128)), ("p10", (128, 256)), ("sel", (128, 128)), ("spr", (128, 512))):
         made.append((name, vmem(*shape, kind=BF16)))
     made.append(("load", pltpu.SemaphoreType.DMA((3,))))

time: 44.3 us -> 42.5 us (0.959)
  Pallas kernels: 43.6 us -> 41.7 us
    pallas_call x1, Pallas kernels: 43.6 us -> 41.7 us  [shards(): pl.pallas_call(kernel, out_shape=jax.ShapeDtypeStruct(concentration.shape...]
where the time goes in v3:
time: 42.5 us; the launch traced here: 42.4 us
  Pallas kernels  41.7 us (98%)
  local copies, waits for them, and re-layouts  0.66 us (2%)
    pallas_call x1, Pallas kernels, shards(): pl.pallas_call(kernel, out_shape=jax.ShapeDtypeStruct(concentration.shape...  41.7 us

profile of v3, /device:TPU:1, one launch (start us, length us, event | category | flops | bytes accessed | tf_op | source)
XLA Modules:
  0.0 42.4 jit_solution(2804628380173920408)
XLA Ops:
  0.0 41.7 %vcycle.1 = f32[8,16,256]{2,1,0:T(8,128)S(1)} custom-call(f32[8,16,256]{2,1,0:T(8,128)} %conc.1, f32[8,16,256]{2,1,0:T(8,128)} %source.1, s32[8,16,256]{2,1,0:T(8,128)} %material.1), custom_call_target="tpu_custom_call" | custom-call | flops 20000000 | bytes 1000000 | tf_op jit(solution)/shard_map/vcycle/pallas_call | solution.py:621
  41.7 0.7 %copy.5 = f32[8,16,256]{2,1,0:T(8,128)} copy(f32[8,16,256]{2,1,0:T(8,128)S(1)} %vcycle.1) | data formatting | bytes 262144

commit v4 on v3

--- a/solution.py
+++ b/solution.py
@@ -192,14 +192,14 @@
         pltpu.make_async_copy(conc, s["va"].at[3:11, 0:16], s["load"].at[1]),
         pltpu.make_async_copy(source, s["src"].at[3:11, 0:16], s["load"].at[2]),
     ]
-    for c in loads:
-        c.start()
     barrier = pltpu.get_barrier_semaphore()
     peers = [(d, 0) for d in range(1, N)] + [(0, d) for d in range(1, N)]
     peers += [(a, b) for a in (-2, -1, 1, 2) for b in (-1, 1)]
     peers.sort(key=lambda p: -min(p[0] % N, -p[0] % N) - min(p[1] % N, -p[1] % N))
     for p in peers:
         pl.semaphore_signal(barrier, inc=1, device_id=device(*p), device_id_type=MESH)
+    for c in loads:
+        c.start()
 
     loads[0].wait()
     k0 = s["k0"]
@@ -238,10 +238,10 @@
     edges0("hs", s["src"], 2)
     pl.semaphore_wait(barrier, len(peers))
 
-    def merge0(group, dest, w):
+    def merge0(group, dest, w, layers=range(14)):
         below = s[group + "_b"]
         row = iota((8, 256), 0)
-        for x in range(14):
+        for x in layers:
             dest[x, 16:24] = jnp.where(row < 4, dest[x, 16:24], roll(below[x], -w, 0))
 
     in_k0 = halo0("hk", k0, k0, 3, 2)
@@ -350,23 +350,31 @@
         for x in range(14):
             dest[x] = ref[x].reshape(20, 128)[2:18]
 
-    in_k1 = halo1("h1k", k1, 7)
     in_ka = ring_x("ka", s["ka"], s["kt"], base)
     in_k2a = window_x("k2a", x2k)
     arrive(in_k0)
     merge0("hk", k0, 3)
     make_ops(k0, ops0, 1.0, 14, 13)
-    arrive(in_va)
-    arrive(in_src)
-    merge0("hv", s["va"], 3)
-    merge0("hs", s["src"], 2)
+    in_k1 = halo1("h1k", k1, 7)
+    arrive(in_va[2:4])
+    arrive(in_src[2:4])
+    merge0("hv", s["va"], 3, range(3, 11))
+    merge0("hs", s["src"], 2, range(3, 11))
     va, vb, vc, vd, ve, src, g0 = [s[name] for name in ("va", "vb", "vc", "vd", "ve", "src", "g0")]
 
     def force(x):
         g0[x] = RATE * va[x] + src[x]
 
-    each(1, 13, 12, force)
-    sweep(va, vb, g0, ops0, 1, 13, 12)
+    each(3, 11, 8, force)
+    sweep(va, vb, g0, ops0, 4, 10, 6)
+    arrive(in_va[:2] + in_va[4:])
+    arrive(in_src[:2] + in_src[4:])
+    merge0("hv", va, 3, (0, 1, 2, 11, 12, 13))
+    merge0("hs", src, 2, (1, 2, 11, 12))
+    for x in (1, 2, 11, 12):
+        force(x)
+    sweep(va, vb, g0, ops0, 1, 4, 3)
+    sweep(va, vb, g0, ops0, 10, 13, 3)
     sweep(vb, vc, g0, ops0, 2, 12, 10)
 
     def down0(c):
@@ -390,6 +398,9 @@
 
     arrive(in_k1)
     make_ops(k1, ops1, 0.25, 18, 17)
+    arrive(in_k2b)
+    window(x2k, k2)
+    make_ops(k2, ops2, 0.0625, 14, 13)
     arrive(in_f1)
 
     v1a, v1b = s["v1a"], s["v1b"]
@@ -407,9 +418,6 @@
     for c in range(2):
         x2f[6 + c, 2] = low[8 * c + 18 : 8 * c + 22]
 
-    arrive(in_k2b)
-    window(x2k, k2)
-    make_ops(k2, ops2, 0.0625, 14, 13)
     v2a, v2b = s["v2a"], s["v2b"]
     near = [[ref[x, 4:12] for x in range(4, 10)] for ref in ops2]
     fl = [f2l[c] for c in range(6)]

time: 42.5 us -> 41.7 us (0.981)
  Pallas kernels: 41.7 us -> 40.9 us
    pallas_call x1, Pallas kernels: 41.7 us -> 40.9 us  [shards(): pl.pallas_call(kernel, out_shape=jax.ShapeDtypeStruct(concentration.shape...]
where the time goes in v4:
time: 41.7 us; the launch traced here: 41.6 us
  Pallas kernels  40.9 us (98%)
  local copies, waits for them, and re-layouts  0.66 us (2%)
    pallas_call x1, Pallas kernels, shards(): pl.pallas_call(kernel, out_shape=jax.ShapeDtypeStruct(concentration.shape...  40.9 us

profile of v4, /device:TPU:1, one launch (start us, length us, event | category | flops | bytes accessed | tf_op | source)
XLA Modules:
  0.0 41.6 jit_solution(4382710635710399812)
XLA Ops:
  0.0 40.9 %vcycle.1 = f32[8,16,256]{2,1,0:T(8,128)S(1)} custom-call(f32[8,16,256]{2,1,0:T(8,128)} %conc.1, f32[8,16,256]{2,1,0:T(8,128)} %source.1, s32[8,16,256]{2,1,0:T(8,128)} %material.1), custom_call_target="tpu_custom_call" | custom-call | flops 20000000 | bytes 1000000 | tf_op jit(solution)/shard_map/vcycle/pallas_call | solution.py:629
  40.9 0.7 %copy.5 = f32[8,16,256]{2,1,0:T(8,128)} copy(f32[8,16,256]{2,1,0:T(8,128)S(1)} %vcycle.1) | data formatting | bytes 262144

commit v5 on v4

--- a/solution.py
+++ b/solution.py
@@ -320,7 +320,7 @@
     def ring_x(group, ref, tile_ref, value):
         tile_ref[...] = value
         ref[me_x] = value
-        return [copy(group, tile_ref, ref.at[me_x], d, 0) for d in range(1, N)]
+        return [copy(group, tile_ref, ref.at[me_x], d, 0) for d in (4, 12, 3, 5, 11, 13, 2, 6, 10, 14, 8, 7, 9, 1, 15)]
 
     def window_x(group, ref):
         return [
@@ -341,7 +341,7 @@
         for k in range(4):
             slab_ref[k] = parts[k]
             ref[k, me_y] = parts[k]
-        return [copy(group, slab_ref, ref.at[:, me_y], 0, d) for d in range(1, N)]
+        return [copy(group, slab_ref, ref.at[:, me_y], 0, d) for d in (12, 4, 5, 11, 13, 3, 10, 6, 8, 14, 2, 7, 9, 15, 1)]
 
     def window_y(group, ref):
         return [copy(group, ref.at[:, 2], ref.at[:, 2 - d], 0, d) for d in (1, -1, 2, -2)]
@@ -401,6 +401,13 @@
     arrive(in_k2b)
     window(x2k, k2)
     make_ops(k2, ops2, 0.0625, 14, 13)
+    near = s["near"]
+    for c in range(6):
+        a, am, b, d, w = [ref[x, 4:12] for ref, x in zip((ops2[0], ops2[0], ops2[1], ops2[2], ops2[3]), (c + 4, c + 3, c + 4, c + 4, c + 4))]
+        bm, dm = roll(b, 1, 0), roll(d, 1, 1)
+        diag = (RATE + a + am) + (b + bm) + (d + dm)
+        for number, value in enumerate((w * a, w * am, w * b, w * bm, w * d, w * dm, w, diag * (1.0 / RELAX))):
+            near[c, number] = value
     arrive(in_f1)
 
     v1a, v1b = s["v1a"], s["v1b"]
@@ -419,15 +426,17 @@
         x2f[6 + c, 2] = low[8 * c + 18 : 8 * c + 22]
 
     v2a, v2b = s["v2a"], s["v2b"]
-    near = [[ref[x, 4:12] for x in range(4, 10)] for ref in ops2]
-    fl = [f2l[c] for c in range(6)]
-    vl = [near[3][c] * fl[c] for c in range(6)]
-
-    def res_near(v, c):
-        return residual(v[c], v[c - 1], v[c + 1], fl[c], near[0][c], near[0][c - 1], near[1][c], near[2][c])
-
-    ul = [None] + [vl[c] + near[3][c] * res_near(vl, c) for c in range(1, 5)]
-    base = to_level3(res_near(ul + [None], 2) + res_near(ul + [None], 3), 2)
+    vl = [near[c, 6] * f2l[c] for c in range(6)]
+
+    def step_near(v, c):
+        o, u = [near[c, number] for number in range(6)], v[c]
+        along_x = o[0] * v[c + 1] + o[1] * v[c - 1]
+        along_y = o[2] * roll(u, -1, 0) + o[3] * roll(u, 1, 0)
+        along_z = o[4] * roll(u, -1, 1) + o[5] * roll(u, 1, 1)
+        return (along_x + along_y) + (along_z + (vl[c] - RELAX * u))
+
+    ul = [None] + [vl[c] + step_near(vl, c) for c in range(1, 5)] + [None]
+    base = to_level3(near[2, 7] * step_near(ul, 2) + near[3, 7] * step_near(ul, 3), 2)
     in_fa = ring_x("fa", s["fa"], s["ft"], base)
     in_f2a = window_x("f2a", x2f)
 
@@ -592,6 +601,7 @@
         made.append((name + "_e", vmem(8, 8, 256)))
         made.append((name + "_b", vmem(14, 8, 256)))
     made.append(("f2l", vmem(6, 8, 128)))
+    made.append(("near", vmem(6, 8, 8, 128)))
     for name in ("ka", "fa"):
         made.append((name, vmem(N, 2, 128)))
     for name in ("kb", "fb"):

time: 41.7 us -> 41.2 us (0.988)
    pallas_call x1, Pallas kernels: 40.9 us -> 40.5 us  [shards(): pl.pallas_call(kernel, out_shape=jax.ShapeDtypeStruct(concentration.shape...]
where the time goes in v5:
time: 41.2 us; the launch traced here: 41.1 us
  Pallas kernels  40.5 us (98%)
  local copies, waits for them, and re-layouts  0.66 us (2%)
    pallas_call x1, Pallas kernels, shards(): pl.pallas_call(kernel, out_shape=jax.ShapeDtypeStruct(concentration.shape...  40.5 us

profile of v5, /device:TPU:1, one launch (start us, length us, event | category | flops | bytes accessed | tf_op | source)
XLA Modules:
  0.0 41.1 jit_solution(7128009990448449142)
XLA Ops:
  0.0 40.5 %vcycle.1 = f32[8,16,256]{2,1,0:T(8,128)S(1)} custom-call(f32[8,16,256]{2,1,0:T(8,128)} %conc.1, f32[8,16,256]{2,1,0:T(8,128)} %source.1, s32[8,16,256]{2,1,0:T(8,128)} %material.1), custom_call_target="tpu_custom_call" | custom-call | flops 20000000 | bytes 1000000 | tf_op jit(solution)/shard_map/vcycle/pallas_call | solution.py:639
  40.5 0.7 %copy.5 = f32[8,16,256]{2,1,0:T(8,128)} copy(f32[8,16,256]{2,1,0:T(8,128)S(1)} %vcycle.1) | data formatting | bytes 262144

commit v6 on v5

--- a/solution.py
+++ b/solution.py
@@ -255,11 +255,6 @@
     matrix("r01", lambda i, j: i // 2 == j)
     matrix("r12", lambda i, j: i // 2 == j % 64)
     matrix("r23", lambda i, j: i // 2 == j // 4)
-    matrix("p32", lambda i, j: i // 4 == (j % 64) // 2)
-    matrix("p21", lambda i, j: i == j // 2)
-    matrix("p10", lambda i, j: i == j // 2)
-    matrix("sel", lambda i, j: ((i % 32) // 4 < 4) & (i % 2 == 0) & (j == ((i % 32) // 4) * 8 + (i // 32) * 2 + (i % 4) // 2))
-    matrix("spr", lambda i, j: i == (j // 128) * 8 + ((j % 128) // 32) * 2 + (j % 4) // 2)
 
     t0, t1, t2 = s["t0"], s["t1"], s["t2"]
 
@@ -352,6 +347,12 @@
 
     in_ka = ring_x("ka", s["ka"], s["kt"], base)
     in_k2a = window_x("k2a", x2k)
+    matrix("p32", lambda i, j: i // 4 == (j % 64) // 2)
+    matrix("p21", lambda i, j: i == j // 2)
+    matrix("p10", lambda i, j: i == j // 2)
+    matrix("sel", lambda i, j: ((i % 32) // 4 < 4) & (i % 2 == 0) & (j == ((i % 32) // 4) * 8 + (i // 32) * 2 + (i % 4) // 2))
+    matrix("spr", lambda i, j: i == (j // 128) * 8 + ((j % 128) // 32) * 2 + (j % 4) // 2)
+
     arrive(in_k0)
     merge0("hk", k0, 3)
     make_ops(k0, ops0, 1.0, 14, 13)

time: 41.2 us -> 41.2 us (level)
  no operation moved by 1% of the time
where the time goes in v6:
time: 41.2 us; the launch traced here: 41.1 us
  Pallas kernels  40.5 us (98%)
  local copies, waits for them, and re-layouts  0.66 us (2%)
    pallas_call x1, Pallas kernels, shards(): pl.pallas_call(kernel, out_shape=jax.ShapeDtypeStruct(concentration.shape...  40.5 us

profile of v6, /device:TPU:1, one launch (start us, length us, event | category | flops | bytes accessed | tf_op | source)
XLA Modules:
  0.0 41.1 jit_solution(1580275162050243517)
XLA Ops:
  0.0 40.5 %vcycle.1 = f32[8,16,256]{2,1,0:T(8,128)S(1)} custom-call(f32[8,16,256]{2,1,0:T(8,128)} %conc.1, f32[8,16,256]{2,1,0:T(8,128)} %source.1, s32[8,16,256]{2,1,0:T(8,128)} %material.1), custom_call_target="tpu_custom_call" | custom-call | flops 20000000 | bytes 1000000 | tf_op jit(solution)/shard_map/vcycle/pallas_call | solution.py:640
  40.5 0.7 %copy.5 = f32[8,16,256]{2,1,0:T(8,128)} copy(f32[8,16,256]{2,1,0:T(8,128)S(1)} %vcycle.1) | data formatting | bytes 262144

commit v7 on v6

--- a/solution.py
+++ b/solution.py
@@ -392,10 +392,6 @@
     in_k2b = window_y("k2b", x2k)
     arrive(in_ka)
     in_kb = ring_y("kb", s["kb"], s["ks"], slab(s["ka"]))
-    stay = pltpu.make_async_copy(vc.at[tile0], vd.at[tile0], s["load"].at[0])
-    stay.start()
-    edges0("hd", vc, 2)
-    in_vd = halo0("hd", vc, vd, 2, 1)
 
     arrive(in_k1)
     make_ops(k1, ops1, 0.25, 18, 17)
@@ -479,6 +475,10 @@
     in_fb = ring_y("fb", s["fb"], s["fs"], slab(s["fa"]))
     arrive(in_f2a)
     in_f2b = window_y("f2b", x2f)
+    stay = pltpu.make_async_copy(vc.at[tile0], vd.at[tile0], s["load"].at[0])
+    stay.start()
+    edges0("hd", vc, 2)
+    in_vd = halo0("hd", vc, vd, 2, 1)
     lax.fori_loop(16, 32, eliminate, 0)
     inverse = roll(m_ref[...], -32, 1)
     inverse = jnp.concatenate([jnp.where(p < 32, inverse, 0.0), jnp.zeros((96, 128), F32)], axis=0)

time: 41.2 us -> 41.4 us (level)
  no operation moved by 1% of the time
where the time goes in v7:
time: 41.4 us
  Pallas kernels  40.7 us (98%)
  local copies, waits for them, and re-layouts  0.66 us (2%)
    pallas_call x1, Pallas kernels, shards(): pl.pallas_call(kernel, out_shape=jax.ShapeDtypeStruct(concentration.shape...  40.7 us

profile of v7, /device:TPU:1, one launch (start us, length us, event | category | flops | bytes accessed | tf_op | source)
XLA Modules:
  0.0 41.4 jit_solution(1704084504678699440)
XLA Ops:
  0.0 40.7 %vcycle.1 = f32[8,16,256]{2,1,0:T(8,128)S(1)} custom-call(f32[8,16,256]{2,1,0:T(8,128)} %conc.1, f32[8,16,256]{2,1,0:T(8,128)} %source.1, s32[8,16,256]{2,1,0:T(8,128)} %material.1), custom_call_target="tpu_custom_call" | custom-call | flops 20000000 | bytes 1000000 | tf_op jit(solution)/shard_map/vcycle/pallas_call | solution.py:640
  40.7 0.7 %copy.5 = f32[8,16,256]{2,1,0:T(8,128)} copy(f32[8,16,256]{2,1,0:T(8,128)S(1)} %vcycle.1) | data formatting | bytes 262144
